TPU v7x, 256 devices: a whole 4x4x8 slice. The times are simulated.
256 devices in a mesh: qrow: 32 (over z_hi, y, core), kcol: 8 (over z_lo, x).
Axes of the slice: x: 4, y: 4, z: 8 (z_hi: 4, z_lo: 2; z = z_hi * 2 + z_lo), core: 2. Of those that a mesh axis runs over, the one named last changes fastest.
Arguments:
- queries: bfloat16 [32768, 256], P(('qrow', 'kcol'))
- keys: bfloat16 [32768, 128], P(('qrow', 'kcol'))
- values: bfloat16 [32768, 128], P(('qrow', 'kcol'))
- out_grad: bfloat16 [32768, 256], P(('qrow', 'kcol'))
- outputs: bfloat16 [32768, 256], P(('qrow', 'kcol')), as said below
- log_norm: float32 [2, 32768], P(None, ('qrow', 'kcol')), as said below
- perm_blocks: int32 [256], replicated, may hold values from 0 to 255, as said below
- doc_bounds: int32 [16], replicated, may hold values from 0 to 32767, as said below
- block_map: int32 [256, 256], replicated, may hold values from 0 to 1, as said below
Outputs:
- grad_query: float32 [32768, 256], P(('qrow', 'kcol'))
- grad_key: float32 [32768, 128], P(('qrow', 'kcol'))
- grad_value: float32 [32768, 128], P(('qrow', 'kcol'))
Inputs may be any that keep to these rules, and one draw needn't show every extreme that they name: `perm_blocks`: every sequence block appears once. `doc_bounds`: strictly increasing, the first entry 0. `block_map`: an entry is 1 exactly where some token of the first block may attend some token of the second under the causal document mask, else 0. `log_norm`: for each head and query, the log of the sum of exp(scores) over the keys it is allowed, with the given queries and keys. `outputs`: the forward attention output of the given queries, keys and values under the same mask, rounded to bfloat16.
All inputs are finite; a program needn't handle non-finite values.
Results may differ from a plain program's by a relative error of at most 0.0029.
Values may be sent and summed in bfloat16 or wider, within the bound.
No kernel may reach another device: no remote copies, remote signals or barrier semaphores. Data moves between devices by JAX's collectives and lax.ppermute only.
A program may use at most 128 MiB of HBM per device.

v0:
```python
import jax
import jax.numpy as jnp
import numpy as np
from jax import lax
from jax.experimental import pallas as pl
from jax.experimental.pallas import tpu as pltpu
from jax.sharding import PartitionSpec as P

AXES = ("qrow", "kcol")
LOG2E = 1.4426950408889634
TOK = 128
AUX = 16
QROWS = 4 * TOK + AUX
GROUP = 16
HALF = GROUP // 2
PARTS = ((0, 8), (12, 16), (8, 12))
LISTS, LIST = 8, GROUP * HALF // 2 + 8
UNROLL = (2, 2, 2)


def coords(i):
    return (i // 64) * 2 + (i // 4) % 2, (i // 16) % 4, (i // 8) % 2, i % 4


def index(z, y, core, x):
    return (((z // 2) * 4 + y) * 2 + core) * 8 + (z % 2) * 4 + x


def pair4(i, flip):
    return 3 - i if flip else i ^ 1


def pair_z(z, y, c, x):
    return 2 * pair4(z // 2, False) + z % 2, y, c, x


def pair_core(z, y, c, x):
    return z, y, 1 - c, x


def pair_z1(z, y, c, x):
    return 2 * pair4(z // 2, True) + z % 2, y, c, x


def pair_z2(z, y, c, x):
    return z ^ 1, y, c, x


def pair_x1(z, y, c, x):
    return z, y, c, pair4(x, c == 1)


def pair_x2(z, y, c, x):
    return z, y, c, pair4(x, c == 0)


def pair_z3(z, y, c, x):
    return pair_z1(*pair_z2(z, y, c, x))


def pair_y1(z, y, c, x):
    return z, pair4(y, c == 1), c, x


def pair_y2(z, y, c, x):
    return z, pair4(y, c == 0), c, x


def partners(pair):
    return np.array([index(*pair(*coords(i))) for i in range(256)])


def joined(pairs):
    table = np.arange(256)[:, None]
    for pair in pairs:
        table = np.concatenate([table, table[partners(pair)]], axis=1)
    return table


def swap(value, pair):
    to = partners(pair)
    return lax.ppermute(value, AXES, [(i, int(to[i])) for i in range(256)])


def slot_tables():
    queries = joined([pair_z, pair_x1, pair_x2, pair_core])
    keys = joined([pair_z1, pair_z2, pair_y1, pair_y2])
    return np.concatenate([queries, keys], axis=1).astype(np.int32)


def prep_kernel(q_ref, g_ref, o_ref, n_ref, k_ref, v_ref, qpay_ref, kvpay_ref):
    rows = [n_ref[0:1, :], n_ref[1:2, :]]
    for head in range(2):
        cols = slice(head * TOK, (head + 1) * TOK)
        qpay_ref[0, head * TOK : (head + 1) * TOK, :] = q_ref[:, cols]
        qpay_ref[0, (2 + head) * TOK : (3 + head) * TOK, :] = g_ref[:, cols]
        product = g_ref[:, cols].astype(jnp.float32) * o_ref[:, cols].astype(jnp.float32)
        rows.append(jnp.sum(product.T, axis=0, keepdims=True))
    exact = jnp.concatenate(rows, axis=0)
    high = exact.astype(jnp.bfloat16).astype(jnp.float32)
    rest = exact - high
    mid = rest.astype(jnp.bfloat16).astype(jnp.float32)
    low = rest - mid
    parts = jnp.concatenate([high, mid, low, jnp.zeros_like(low)], axis=0)
    qpay_ref[0, 4 * TOK :, :] = parts.astype(jnp.bfloat16)
    kvpay_ref[0, 0:TOK, :] = k_ref[...]
    kvpay_ref[0, TOK:, :] = v_ref[...]


def list_kernel(perm_ref, bounds_ref, ids_ref, list_ref, base_ref, rows_ref):
    lane = lax.broadcasted_iota(jnp.int32, (1, TOK), 1)
    for slot in range(GROUP):
        base_ref[slot] = perm_ref[ids_ref[GROUP + slot]] * TOK
        first = perm_ref[ids_ref[slot]] * TOK
        position = first + lane
        start = jnp.zeros((1, TOK), jnp.int32)
        first_start = jnp.int32(0)
        for doc in range(16):
            bound = bounds_ref[doc]
            start = jnp.where(position >= bound, bound, start)
            first_start = jnp.where(first >= bound, bound, first_start)
        base_ref[GROUP + 1 + slot] = first
        base_ref[2 * GROUP + 1 + slot] = first_start
        rows_ref[slot, 0:1, :] = start
        rows_ref[slot, 1:2, :] = position
    base_ref[GROUP] = jnp.int32(-(1 << 20))

    for part, (begin, end) in enumerate(PARTS):
        place = LISTS + part * LIST

        def outer(qs, count):
            first, first_start = base_ref[GROUP + 1 + qs], base_ref[2 * GROUP + 1 + qs]
            held = jnp.int32(GROUP)
            for ks in range(begin, end):
                base = base_ref[ks]
                active = (base <= first) & (first_start <= base + (TOK - 1))
                full = held != GROUP
                entry = qs + 16 * jnp.where(full, held + 32 * ks, ks + 32 * GROUP)
                list_ref[jnp.where(active, place + count, 0)] = entry
                count = count + (active & full).astype(jnp.int32)
                held = jnp.where(active, jnp.where(full, GROUP, ks), held)
            return count + (held != GROUP).astype(jnp.int32)

        count = lax.fori_loop(0, GROUP, outer, jnp.int32(0))
        list_ref[1 + part] = count
        for extra in range(UNROLL[part] - 1):
            list_ref[place + count + extra] = jnp.int32(16 * (GROUP + 32 * GROUP))


def join_kernel(a0, a1, b0, b1, a_ref, b_ref):
    for first, second, ref in ((a0, a1, a_ref), (b0, b1, b_ref)):
        split = first.shape[0]
        ref[0:split] = first[...]
        ref[split:] = second[...]


def hold_kernel(a0, b0, a_ref, b_ref):
    a_ref[...] = a0[...]
    b_ref[...] = b0[...]


def finish_kernel(g_ref, g1, g2, g3, dq_ref, dq_in, query_ref, key_ref, value_ref):
    for ref, rows in ((key_ref, slice(0, TOK)), (value_ref, slice(TOK, 2 * TOK))):
        total = g_ref[0, rows, :]
        for part in (g1, g2, g3):
            total = total + part[0, rows, :].astype(jnp.float32)
        ref[...] = total
    for head in range(2):
        cols = slice(head * TOK, (head + 1) * TOK)
        query_ref[:, cols] = (dq_ref[0, :, cols] + dq_in[0, :, cols].astype(jnp.float32)).T


NT = (((1,), (1,)), ((), ()))


def walk(part, list_ref, base_ref, rows_ref, q_all, aux, kv_refs, kv_all, kt, dq, dkv):
    scale = TOK ** (-0.5)
    begin = PARTS[part][0]
    unroll = UNROLL[part]
    place = LISTS + part * LIST
    sub = lax.broadcasted_iota(jnp.int32, (TOK, TOK), 0)
    for slot in range(PARTS[part][1] - begin):
        block = kv_refs[slot // 4][slot % 4]
        kv_all[slot] = block
        kt[slot] = block[0:TOK, :].T
    dkv[...] = jnp.zeros_like(dkv)

    def tiles(entry):
        qs = entry & (GROUP - 1)
        slots = [(entry >> shift) & 31 for shift in (4, 9)]
        places = [jnp.where(slot == GROUP, 0, slot - begin) for slot in slots]
        bases = [base_ref[slot] for slot in slots]
        q = q_all[qs, 0 : 2 * TOK, :]
        g = q_all[qs, 2 * TOK : 4 * TOK, :]
        k = jnp.concatenate([kv_all[at, 0:TOK, :] for at in places], axis=0)
        v = jnp.concatenate([kv_all[at, TOK:, :] for at in places], axis=0)
        scores = lax.dot_general(k, q, NT, preferred_element_type=jnp.float32)
        dprob = lax.dot_general(v, g, NT, preferred_element_type=jnp.float32)
        start, position = rows_ref[qs, 0:1, :], rows_ref[qs, 1:2, :]
        allowed = [(sub >= start - base) & (sub <= position - base) for base in bases]
        allowed = jnp.concatenate([jnp.concatenate([part, part], axis=1) for part in allowed], axis=0)
        weights = jnp.where(allowed, jnp.exp2(scores * (scale * LOG2E) - aux[qs, 0:1, :]), 0.0)
        dscore = (weights * (dprob - aux[qs, 1:2, :]) * scale).astype(jnp.bfloat16)
        dv = jnp.dot(weights.astype(jnp.bfloat16), g, preferred_element_type=jnp.float32)
        dk = jnp.dot(dscore, q, preferred_element_type=jnp.float32)
        k_t = jnp.concatenate([kt[at] for at in places], axis=1)
        dqt = jnp.dot(k_t, dscore, preferred_element_type=jnp.float32)
        return qs, places, dqt, dk, dv

    def step(i, carry):
        done = [tiles(list_ref[place + unroll * i + j]) for j in range(unroll)]
        for qs, places, dqt, dk, dv in done:
            for at, rows in zip(places, (slice(0, TOK), slice(TOK, 2 * TOK))):
                dkv[at, TOK:, :] += dv[rows]
                dkv[at, 0:TOK, :] += dk[rows]
            dq[qs] += dqt
        return carry

    lax.fori_loop(0, (list_ref[1 + part] + (unroll - 1)) // unroll, step, 0)


def first_kernel(list_ref, base_ref, rows_ref, q0, q1, q2, q3, kv0, kv1, q_all, aux, dq, dkv, kv_all, kt):
    for part, q_ref in enumerate((q0, q1, q2, q3)):
        q_all[4 * part : 4 * part + 4] = q_ref[...]
        for slot in range(4):
            parts = q_ref[slot, 4 * TOK :, :].astype(jnp.float32)
            exact = (parts[8:12] + parts[4:8]) + parts[0:4]
            for head in range(2):
                cols = slice(head * TOK, (head + 1) * TOK)
                aux[4 * part + slot, 0:1, cols] = exact[head : head + 1] * LOG2E
                aux[4 * part + slot, 1:2, cols] = exact[2 + head : 3 + head]
    dq[...] = jnp.zeros_like(dq)
    walk(0, list_ref, base_ref, rows_ref, q_all, aux, (kv0, kv1), kv_all, kt, dq, dkv)


def far_kernel(list_ref, base_ref, rows_ref, q_all, aux, before, kv_ref, dq, out_ref, dkv, kv_all, kt):
    dq[...] = before[...]
    walk(1, list_ref, base_ref, rows_ref, q_all, aux, (kv_ref,), kv_all, kt, dq, dkv)
    out_ref[...] = dkv[...].astype(jnp.bfloat16)


def last_kernel(list_ref, base_ref, rows_ref, q_all, aux, before, kv_ref, dqa_ref, *refs):
    outs, (out_ref, dq, dkv, kv_all, kt) = refs[:4], refs[4:]
    dq[...] = before[...]
    walk(2, list_ref, base_ref, rows_ref, q_all, aux, (kv_ref,), kv_all, kt, dq, dkv)
    dqa_ref[...] = dq[0:HALF]
    for i, ref in enumerate(outs):
        ref[...] = dq[HALF + 2 * i : HALF + 2 * i + 2].astype(jnp.bfloat16)
    out_ref[...] = dkv[...].astype(jnp.bfloat16)


def spec(space=pltpu.VMEM):
    return pl.BlockSpec(memory_space=space)


def together(*arrays):
    return lax.optimization_barrier(arrays)


def whole(array):
    return pl.BlockSpec(array.shape, lambda i: (0, 0))


def body(queries, keys, values, out_grad, outputs, log_norm, perm_blocks, doc_bounds, block_map):
    del block_map
    me = lax.axis_index("qrow") * lax.axis_size("kcol") + lax.axis_index("kcol")
    ids = jnp.asarray(slot_tables())[me]
    params = pltpu.CompilerParams(vmem_limit_bytes=40 * 1024 * 1024)
    q1, kv1 = pl.pallas_call(
        prep_kernel,
        out_shape=(
            jax.ShapeDtypeStruct((1, QROWS, TOK), jnp.bfloat16),
            jax.ShapeDtypeStruct((1, 2 * TOK, TOK), jnp.bfloat16),
        ),
        grid=(1,),
        in_specs=[whole(a) for a in (queries, out_grad, outputs, log_norm, keys, values)],
        out_specs=(spec(), spec()),
        compiler_params=pltpu.CompilerParams(vmem_limit_bytes=60 * 1024 * 1024),
        name="prep",
    )(queries, out_grad, outputs, log_norm, keys, values)
    tiles, bases, rows = pl.pallas_call(
        list_kernel,
        out_shape=(
            jax.ShapeDtypeStruct((LISTS + 3 * LIST,), jnp.int32),
            jax.ShapeDtypeStruct((64,), jnp.int32),
            jax.ShapeDtypeStruct((GROUP, 8, TOK), jnp.int32),
        ),
        in_specs=[spec(pltpu.SMEM)] * 3,
        out_specs=(spec(pltpu.SMEM), spec(pltpu.SMEM), spec()),
        compiler_params=params,
        name="tiles",
    )(perm_blocks, doc_bounds, ids)

    narrow, wide = jnp.bfloat16, jnp.float32

    def shape(*dims, dtype=wide):
        return jax.ShapeDtypeStruct(dims, dtype)

    def join(q0, q_in, kv0, kv_in):
        n = 2 * q0.shape[0]
        return pl.pallas_call(
            join_kernel,
            out_shape=(shape(n, *q0.shape[1:], dtype=narrow), shape(n, *kv0.shape[1:], dtype=narrow)),
            in_specs=[spec()] * 4,
            out_specs=(spec(),) * 2,
            compiler_params=params,
            name="join",
        )(q0, q_in, kv0, kv_in)

    def compute(kernel, scalars, arrays, outs, scratch, name):
        return pl.pallas_call(
            kernel,
            out_shape=outs,
            in_specs=[spec(pltpu.SMEM)] * 2 + [spec()] * (1 + len(arrays)),
            out_specs=(spec(),) * len(outs),
            scratch_shapes=scratch,
            compiler_params=params,
            cost_estimate=pl.CostEstimate(flops=3 * 10**9, bytes_accessed=10**7, transcendentals=10**6),
            name=name,
        )(*scalars, *arrays)

    held = pl.pallas_call(
        hold_kernel,
        out_shape=(shape(*q1.shape, dtype=narrow), shape(*kv1.shape, dtype=narrow)),
        in_specs=[spec()] * 2,
        out_specs=(spec(),) * 2,
        compiler_params=params,
        name="hold",
    )(q1, kv1)
    q_in, kv_in, q1, kv1 = together(swap(q1, pair_z), swap(kv1, pair_z1), *held)
    q2, kv2 = join(q1, q_in, kv1, kv_in)
    q_in, kv_in = together(swap(q2, pair_x1), swap(kv2, pair_z2))
    q4, kv4 = join(q2, q_in, kv2, kv_in)
    q_x, kv_y1, kv_y2, *scalars = together(
        swap(q4, pair_x2), swap(kv4, pair_y1), swap(kv4, pair_y2), tiles, bases, rows
    )
    q_core, qx_core, kv_far = swap(q4, pair_core), swap(q_x, pair_core), swap(kv_y1, pair_y2)

    def room(slots):
        return [pltpu.VMEM((slots, 2 * TOK, TOK), narrow), pltpu.VMEM((slots, TOK, TOK), narrow)]

    dq_shape, g_rows = (TOK, 2 * TOK), (2 * TOK, TOK)
    q_all, aux, dq, g = compute(
        first_kernel,
        scalars,
        (q4, q_x, q_core, qx_core, kv4, kv_y1),
        (
            shape(GROUP, QROWS, TOK, dtype=narrow),
            shape(GROUP, 8, 2 * TOK),
            shape(GROUP, *dq_shape),
            shape(HALF, *g_rows),
        ),
        room(8),
        "first",
    )
    dq, far = compute(
        far_kernel,
        scalars,
        (q_all, aux, dq, kv_far),
        (shape(GROUP, *dq_shape), shape(4, *g_rows, dtype=narrow)),
        [pltpu.VMEM((4, *g_rows), wide)] + room(4),
        "far",
    )
    dqa, *others, near = compute(
        last_kernel,
        scalars,
        (q_all, aux, dq, kv_y2),
        (shape(HALF, *dq_shape),) + (shape(2, *dq_shape, dtype=narrow),) * 4 + (shape(4, *g_rows, dtype=narrow),),
        [pltpu.VMEM((GROUP, *dq_shape), wide), pltpu.VMEM((4, *g_rows), wide)] + room(4),
        "last",
    )

    far_in, *others = together(swap(far, pair_y2), *[swap(part, pair_core) for part in others])
    b_in, c_in = jnp.concatenate(others[:2]), jnp.concatenate(others[2:])
    far = g[4:] + far_in.astype(wide)
    near_in, far_in, dq_in = together(
        swap(near, pair_y2), swap(far.astype(narrow), pair_y1), swap((dqa[4:] + c_in.astype(wide)).astype(narrow), pair_x2)
    )
    g, dq = (g[:4] + near_in.astype(wide)) + far_in.astype(wide), (dqa[:4] + b_in.astype(wide)) + dq_in.astype(wide)
    g_in = [swap(g[i : i + 1].astype(narrow), pair) for i, pair in enumerate((pair_z1, pair_z2, pair_z3), 1)]
    dq = dq[:2] + swap(dq[2:].astype(narrow), pair_x1).astype(wide)
    dq_in = swap(dq[1:].astype(narrow), pair_z)
    return pl.pallas_call(
        finish_kernel,
        out_shape=(shape(TOK, 2 * TOK), shape(TOK, TOK), shape(TOK, TOK)),
        in_specs=[spec()] * 6,
        out_specs=(spec(),) * 3,
        compiler_params=params,
        name="finish",
    )(g, *g_in, dq, dq_in)


def solution(mesh):
    rows, cols = P(AXES, None), P(None, AXES)
    return jax.shard_map(
        body,
        mesh=mesh,
        in_specs=(rows, rows, rows, rows, rows, cols, P(), P(), P()),
        out_specs=(rows, rows, rows),
        check_vma=False,
    )
```

profile of v0, /device:TPU:2, one launch (start us, length us, event | category | flops | bytes accessed | tf_op | source)
XLA Modules:
  0.0 74.1 jit_solution(4950313542379799368)
XLA Ops:
  0.6 1.7 %prep.1 = (bf16[1,528,128]{2,1,0:T(8,128)(2,1)}, bf16[1,256,128]{2,1,0:T(8,128)(2,1)}) custom-call(bf16[128,256]{1,0:T(8,128)(2,1)} %q_ref.1, bf16[128,256]{1,0:T(8,128)(2,1)} %g_ref.1, bf16[128,256]{1,0:T(8,128)(2,1)} %o_ref.1, f32[2,128]{1,0:T(2,128)} %n_ref.1, bf16[128,128]{1,0:T(8,128)(2,1)} %k_ref.1, bf16[128,128]{1,0:T(8,128)(2,1)} %v_ref.1), custom_call_target="tpu_custom_call" | custom-call | tf_op jit(solution)/shard_map/prep/pallas_call | solution.py:269
  2.3 3.3 %collective-permute-start = (bf16[1,528,128]{2,1,0:T(8,128)(2,1)}, bf16[1,528,128]{2,1,0:T(8,128)(2,1)S(1)}, u32[]{:S(2)}, u32[]{:S(2)}) collective-permute-start(bf16[1,528,128]{2,1,0:T(8,128)(2,1)} %get-tuple-element.46.a0), channel_id=1, source_target_pairs={{0,64},{1,65},{2,66},{3,67},{4,68},{5,69},{6,70},{7,71},{8,72},{9,... | collective-permute-start | bytes 405512 | tf_op jit(solution)/shard_map/ppermute | solution.py:82
  5.6 4.5 %collective-permute-start.1 = (bf16[1,256,128]{2,1,0:T(8,128)(2,1)}, bf16[1,256,128]{2,1,0:T(8,128)(2,1)S(1)}, u32[]{:S(2)}, u32[]{:S(2)}) collective-permute-start(bf16[1,256,128]{2,1,0:T(8,128)(2,1)} %get-tuple-element.47.b0), channel_id=1, source_target_pairs={{0,192},{1,193},{2,194},{3,195},{4,196},{5,197},{6,198},{7,199},{8... | collective-permute-start | bytes 196616 | tf_op jit(solution)/shard_map/ppermute | solution.py:82
  10.1 0.9 %copy-done = bf16[1,528,128]{2,1,0:T(8,128)(2,1)S(1)} copy-done((bf16[1,528,128]{2,1,0:T(8,128)(2,1)S(1)}, bf16[1,528,128]{2,1,0:T(8,128)(2,1)}, u32[]{:S(2)}) %copy-start) | copy-done | bytes 135192
  11.0 0.8 %copy-done.1 = bf16[1,256,128]{2,1,0:T(8,128)(2,1)S(1)} copy-done((bf16[1,256,128]{2,1,0:T(8,128)(2,1)S(1)}, bf16[1,256,128]{2,1,0:T(8,128)(2,1)}, u32[]{:S(2)}) %copy-start.1) | copy-done | bytes 65560
  11.8 1.7 %collective-permute-done.1.b1 = bf16[1,256,128]{2,1,0:T(8,128)(2,1)S(1)} collective-permute-done((bf16[1,256,128]{2,1,0:T(8,128)(2,1)}, bf16[1,256,128]{2,1,0:T(8,128)(2,1)S(1)}, u32[]{:S(2)}, u32[]{:S(2)}) %collective-permute-start.1) | collective-permute-done | bytes 65568 | tf_op jit(solution)/shard_map/ppermute | solution.py:82
  13.6 0.6 collective-permute-start.2
  14.2 1.3 %collective-permute-start.3 = (bf16[2,256,128]{2,1,0:T(8,128)(2,1)S(1)}, bf16[2,256,128]{2,1,0:T(8,128)(2,1)S(1)}, u32[]{:S(2)}, u32[]{:S(2)}) collective-permute-start(bf16[2,256,128]{2,1,0:T(8,128)(2,1)S(1)} %get-tuple-element.55.b0), channel_id=1, source_target_pairs={{0,4},{1,5},{2,6},{3,7},{4,0},{5,1},{6,2},{7,3},{8,12},{9,13},{10,... | collective-permute-start | bytes 393224 | tf_op jit(solution)/shard_map/ppermute | solution.py:82
  15.5 3.7 %collective-permute-done.3.b1 = bf16[2,256,128]{2,1,0:T(8,128)(2,1)S(1)} collective-permute-done((bf16[2,256,128]{2,1,0:T(8,128)(2,1)S(1)}, bf16[2,256,128]{2,1,0:T(8,128)(2,1)S(1)}, u32[]{:S(2)}, u32[]{:S(2)}) %collective-permute-start.3) | collective-permute-done | bytes 131104 | tf_op jit(solution)/shard_map/ppermute | solution.py:82
  19.1 1.0 %collective-permute-done.2.a1 = bf16[2,528,128]{2,1,0:T(8,128)(2,1)S(1)} collective-permute-done((bf16[2,528,128]{2,1,0:T(8,128)(2,1)S(1)}, bf16[2,528,128]{2,1,0:T(8,128)(2,1)S(1)}, u32[]{:S(2)}, u32[]{:S(2)}) %collective-permute-start.2) | collective-permute-done | bytes 270368 | tf_op jit(solution)/shard_map/ppermute | solution.py:82
  20.2 1.6 %collective-permute-start.4 = (bf16[4,528,128]{2,1,0:T(8,128)(2,1)S(1)}, bf16[4,528,128]{2,1,0:T(8,128)(2,1)S(1)}, u32[]{:S(2)}, u32[]{:S(2)}) collective-permute-start(bf16[4,528,128]{2,1,0:T(8,128)(2,1)S(1)} %get-tuple-element.58.q0), channel_id=1, source_target_pairs={{0,3},{1,2},{2,1},{3,0},{4,7},{5,6},{6,5},{7,4},{8,9},{9,8},{10,11... | collective-permute-start | bytes 1622024 | tf_op jit(solution)/shard_map/ppermute | solution.py:82
  21.7 1.6 %collective-permute-start.5 = (bf16[4,256,128]{2,1,0:T(8,128)(2,1)S(1)}, bf16[4,256,128]{2,1,0:T(8,128)(2,1)S(1)}, u32[]{:S(2)}, u32[]{:S(2)}) collective-permute-start(bf16[4,256,128]{2,1,0:T(8,128)(2,1)S(1)} %get-tuple-element.59.kv0), channel_id=1, source_target_pairs={{0,16},{1,17},{2,18},{3,19},{4,20},{5,21},{6,22},{7,23},{8,56},{9,... | collective-permute-start | bytes 786440 | tf_op jit(solution)/shard_map/ppermute | solution.py:82
  23.3 2.2 %collective-permute-start.6 = (bf16[4,256,128]{2,1,0:T(8,128)(2,1)S(1)}, bf16[4,256,128]{2,1,0:T(8,128)(2,1)S(1)}, u32[]{:S(2)}, u32[]{:S(2)}) collective-permute-start(bf16[4,256,128]{2,1,0:T(8,128)(2,1)S(1)} %get-tuple-element.59.kv0), channel_id=1, source_target_pairs={{0,48},{1,49},{2,50},{3,51},{4,52},{5,53},{6,54},{7,55},{8,24},{9,... | collective-permute-start | bytes 786440 | tf_op jit(solution)/shard_map/ppermute | solution.py:82
  25.5 0.7 dynamic-slice_bitcast_fusion.ids_ref
  26.2 0.7 copy-done.2
  26.9 0.7 copy-done.3
  27.5 3.1 %tiles.1 = (s32[224]{0:T(256)S(1)}, s32[64]{0:T(128)S(1)}, s32[16,8,128]{2,1,0:T(8,128)S(1)}) custom-call(s32[256]{0:T(256)S(1)} %copy-done.2, s32[16]{0:T(128)S(1)} %copy-done.3, s32[32]{0:T(128)S(1)} %dynamic-slice_bitcast_fusion.ids_ref), custom_call_target="tpu_custom_call" | custom-call | tf_op jit(solution)/shard_map/tiles/pallas_call | solution.py:281
  31.3 1.7 %collective-permute-start.9 = (bf16[4,256,128]{2,1,0:T(8,128)(2,1)S(1)}, bf16[4,256,128]{2,1,0:T(8,128)(2,1)S(1)}, u32[]{:S(2)}, u32[]{:S(2)}) collective-permute-start(bf16[4,256,128]{2,1,0:T(8,128)(2,1)S(1)} %collective-permute-done.5.kv1), channel_id=1, source_target_pairs={{0,48},{1,49},{2,50},{3,51},{4,52},{5,53},{6,54},{7,55},{8,24},{9,... | collective-permute-start | bytes 786440 | tf_op jit(solution)/shard_map/ppermute | solution.py:82
  33.4 4.2 %first.1 = (bf16[16,528,128]{2,1,0:T(8,128)(2,1)S(1)}, f32[16,8,256]{2,1,0:T(8,128)S(1)}, f32[16,128,256]{2,1,0:T(8,128)S(1)}, f32[8,256,128]{2,1,0:T(8,128)S(1)}) custom-call(s32[224]{0:T(256)S(1)} %get-tuple-element.63.list_ref, s32[64]{0:T(128)S(1)} %get-tuple-element.64.base_ref, s32[16,8,128]{2,1,0:T(8,128)S(1)} %get-tuple-element.65.rows_ref, ...), custom_call_target="tpu_custom_call" | custom-call | flops 3000000000 | bytes 10000000 | tf_op jit(solution)/shard_map/first/pallas_call | solution.py:311
  37.7 1.2 %collective-permute-done.9.kv_ref = bf16[4,256,128]{2,1,0:T(8,128)(2,1)S(1)} collective-permute-done((bf16[4,256,128]{2,1,0:T(8,128)(2,1)S(1)}, bf16[4,256,128]{2,1,0:T(8,128)(2,1)S(1)}, u32[]{:S(2)}, u32[]{:S(2)}) %collective-permute-start.9) | collective-permute-done | bytes 262176 | tf_op jit(solution)/shard_map/ppermute | solution.py:82
  38.9 3.4 %far.1 = (f32[16,128,256]{2,1,0:T(8,128)S(1)}, bf16[4,256,128]{2,1,0:T(8,128)(2,1)S(1)}) custom-call(s32[224]{0:T(256)S(1)} %get-tuple-element.63.list_ref, s32[64]{0:T(128)S(1)} %get-tuple-element.64.base_ref, s32[16,8,128]{2,1,0:T(8,128)S(1)} %get-tuple-element.65.rows_ref, bf16[16,528,128]{2,1,0:T(8,128)(2,1)S(1)} %get-tuple-element.69.q_all, ...), custom_call_target="tpu_custom_call" | custom-call | flops 3000000000 | bytes 10000000 | tf_op jit(solution)/shard_map/far/pallas_call | solution.py:311
  42.3 1.8 %collective-permute-start.11 = (bf16[4,256,128]{2,1,0:T(8,128)(2,1)S(1)}, bf16[4,256,128]{2,1,0:T(8,128)(2,1)S(1)}, u32[]{:S(2)}, u32[]{:S(2)}) collective-permute-start(bf16[4,256,128]{2,1,0:T(8,128)(2,1)S(1)} %get-tuple-element.75), channel_id=1, source_target_pairs={{0,48},{1,49},{2,50},{3,51},{4,52},{5,53},{6,54},{7,55},{8,24},{9,... | collective-permute-start | bytes 786440 | tf_op jit(solution)/shard_map/ppermute | solution.py:82
  44.1 3.5 %last.1 = (f32[8,128,256]{2,1,0:T(8,128)S(1)}, bf16[2,128,256]{2,1,0:T(8,128)(2,1)S(1)}, bf16[2,128,256]{2,1,0:T(8,128)(2,1)S(1)}, bf16[2,128,256]{2,1,0:T(8,128...) custom-call(s32[224]{0:T(256)S(1)} %get-tuple-element.63.list_ref, ...), custom_call_target="tpu_custom_call" | custom-call | flops 3000000000 | bytes 10000000 | tf_op jit(solution)/shard_map/last/pallas_call | solution.py:311
  47.7 0.5 collective-permute-start.13
  50.6 8.6 %collective-permute-done.10 = bf16[4,256,128]{2,1,0:T(8,128)(2,1)S(1)} collective-permute-done((bf16[4,256,128]{2,1,0:T(8,128)(2,1)S(1)}, bf16[4,256,128]{2,1,0:T(8,128)(2,1)S(1)}, u32[]{:S(2)}, u32[]{:S(2)}) %collective-permute-start.10) | collective-permute-done | bytes 262176 | tf_op jit(solution)/shard_map/ppermute | solution.py:82
  59.3 1.3 %collective-permute-start.21 = (bf16[2,128,256]{2,1,0:T(8,128)(2,1)S(1)}, bf16[2,128,256]{2,1,0:T(8,128)(2,1)S(1)}, u32[]{:S(2)}, u32[]{:S(2)}) collective-permute-start(bf16[2,128,256]{2,1,0:T(8,128)(2,1)S(1)} %slice.58), channel_id=1, source_target_pairs={{0,1},{1,0},{2,3},{3,2},{4,5},{5,4},{6,7},{7,6},{8,11},{9,10},{10,... | collective-permute-start | bytes 393224 | tf_op jit(solution)/shard_map/ppermute | solution.py:82
  60.7 5.2 %collective-permute-start.18 = (bf16[1,256,128]{2,1,0:T(8,128)(2,1)S(1)}, bf16[1,256,128]{2,1,0:T(8,128)(2,1)S(1)}, u32[]{:S(2)}, u32[]{:S(2)}) collective-permute-start(bf16[1,256,128]{2,1,0:T(8,128)(2,1)S(1)} %get-tuple-element.93), channel_id=1, source_target_pairs={{0,192},{1,193},{2,194},{3,195},{4,196},{5,197},{6,198},{7,199},{8... | collective-permute-start | bytes 196616 | tf_op jit(solution)/shard_map/ppermute | solution.py:82
  65.9 0.7 collective-permute-start.20
  66.6 4.2 %collective-permute-start.22 = (bf16[1,128,256]{2,1,0:T(8,128)(2,1)S(1)}, bf16[1,128,256]{2,1,0:T(8,128)(2,1)S(1)}, u32[]{:S(2)}, u32[]{:S(2)}) collective-permute-start(bf16[1,128,256]{2,1,0:T(8,128)(2,1)S(1)} %slice.59), channel_id=1, source_target_pairs={{0,64},{1,65},{2,66},{3,67},{4,68},{5,69},{6,70},{7,71},{8,72},{9,... | collective-permute-start | bytes 196616 | tf_op jit(solution)/shard_map/ppermute | solution.py:82
  70.8 0.5 collective-permute-done.20.g3
  71.4 2.0 %collective-permute-done.22.dq_in = bf16[1,128,256]{2,1,0:T(8,128)(2,1)S(1)} collective-permute-done((bf16[1,128,256]{2,1,0:T(8,128)(2,1)S(1)}, bf16[1,128,256]{2,1,0:T(8,128)(2,1)S(1)}, u32[]{:S(2)}, u32[]{:S(2)}) %collective-permute-start.22) | collective-permute-done | bytes 65568 | tf_op jit(solution)/shard_map/ppermute | solution.py:82
  73.3 0.8 %finish.1 = (f32[128,256]{1,0:T(8,128)}, f32[128,128]{1,0:T(8,128)}, f32[128,128]{1,0:T(8,128)}) custom-call(f32[4,256,128]{2,1,0:T(8,128)S(1)} %get-tuple-element.90.g_ref, bf16[1,256,128]{2,1,0:T(8,128)(2,1)S(1)} %collective-permute-done.18.g1, bf16[1,256,128]{2,1,0:T(8,128)(2,1)S(1)} %collective-permute-done.19.g2, ...), custom_call_target="tpu_custom_call" | custom-call | tf_op jit(solution)/shard_map/finish/pallas_call | solution.py:383
  (40 shorter events, 3.9 us)
Async XLA Ops:
  2.3 11.2 %collective-permute-start = (bf16[1,528,128]{2,1,0:T(8,128)(2,1)}, bf16[1,528,128]{2,1,0:T(8,128)(2,1)S(1)}, u32[]{:S(2)}, u32[]{:S(2)}) collective-permute-start(bf16[1,528,128]{2,1,0:T(8,128)(2,1)} %get-tuple-element.46.a0), channel_id=1, source_target_pairs={{0,64},{1,65},{2,66},{3,67},{4,68},{5,69},{6,70},{7,71},{8,72},{9,... | collective-permute-start | bytes 405512 | tf_op jit(solution)/shard_map/ppermute | solution.py:82
  5.6 7.9 %collective-permute-start.1 = (bf16[1,256,128]{2,1,0:T(8,128)(2,1)}, bf16[1,256,128]{2,1,0:T(8,128)(2,1)S(1)}, u32[]{:S(2)}, u32[]{:S(2)}) collective-permute-start(bf16[1,256,128]{2,1,0:T(8,128)(2,1)} %get-tuple-element.47.b0), channel_id=1, source_target_pairs={{0,192},{1,193},{2,194},{3,195},{4,196},{5,197},{6,198},{7,199},{8... | collective-permute-start | bytes 196616 | tf_op jit(solution)/shard_map/ppermute | solution.py:82
  10.1 0.9 %copy-start = (bf16[1,528,128]{2,1,0:T(8,128)(2,1)S(1)}, bf16[1,528,128]{2,1,0:T(8,128)(2,1)}, u32[]{:S(2)}) copy-start(bf16[1,528,128]{2,1,0:T(8,128)(2,1)} %get-tuple-element.46.a0) | copy-start | bytes 405508
  11.0 0.8 %copy-start.1 = (bf16[1,256,128]{2,1,0:T(8,128)(2,1)S(1)}, bf16[1,256,128]{2,1,0:T(8,128)(2,1)}, u32[]{:S(2)}) copy-start(bf16[1,256,128]{2,1,0:T(8,128)(2,1)} %get-tuple-element.47.b0) | copy-start | bytes 196612
  13.6 6.5 %collective-permute-start.2 = (bf16[2,528,128]{2,1,0:T(8,128)(2,1)S(1)}, bf16[2,528,128]{2,1,0:T(8,128)(2,1)S(1)}, u32[]{:S(2)}, u32[]{:S(2)}) collective-permute-start(bf16[2,528,128]{2,1,0:T(8,128)(2,1)S(1)} %get-tuple-element.54.a0), channel_id=1, source_target_pairs={{0,1},{1,0},{2,3},{3,2},{4,5},{5,4},{6,7},{7,6},{8,11},{9,10},{10,... | collective-permute-start | bytes 811016 | tf_op jit(solution)/shard_map/ppermute | solution.py:82
  14.2 5.0 %collective-permute-start.3 = (bf16[2,256,128]{2,1,0:T(8,128)(2,1)S(1)}, bf16[2,256,128]{2,1,0:T(8,128)(2,1)S(1)}, u32[]{:S(2)}, u32[]{:S(2)}) collective-permute-start(bf16[2,256,128]{2,1,0:T(8,128)(2,1)S(1)} %get-tuple-element.55.b0), channel_id=1, source_target_pairs={{0,4},{1,5},{2,6},{3,7},{4,0},{5,1},{6,2},{7,3},{8,12},{9,13},{10,... | collective-permute-start | bytes 393224 | tf_op jit(solution)/shard_map/ppermute | solution.py:82
  20.2 10.7 %collective-permute-start.4 = (bf16[4,528,128]{2,1,0:T(8,128)(2,1)S(1)}, bf16[4,528,128]{2,1,0:T(8,128)(2,1)S(1)}, u32[]{:S(2)}, u32[]{:S(2)}) collective-permute-start(bf16[4,528,128]{2,1,0:T(8,128)(2,1)S(1)} %get-tuple-element.58.q0), channel_id=1, source_target_pairs={{0,3},{1,2},{2,1},{3,0},{4,7},{5,6},{6,5},{7,4},{8,9},{9,8},{10,11... | collective-permute-start | bytes 1622024 | tf_op jit(solution)/shard_map/ppermute | solution.py:82
  21.7 9.0 %collective-permute-start.5 = (bf16[4,256,128]{2,1,0:T(8,128)(2,1)S(1)}, bf16[4,256,128]{2,1,0:T(8,128)(2,1)S(1)}, u32[]{:S(2)}, u32[]{:S(2)}) collective-permute-start(bf16[4,256,128]{2,1,0:T(8,128)(2,1)S(1)} %get-tuple-element.59.kv0), channel_id=1, source_target_pairs={{0,16},{1,17},{2,18},{3,19},{4,20},{5,21},{6,22},{7,23},{8,56},{9,... | collective-permute-start | bytes 786440 | tf_op jit(solution)/shard_map/ppermute | solution.py:82
  23.3 7.6 %collective-permute-start.6 = (bf16[4,256,128]{2,1,0:T(8,128)(2,1)S(1)}, bf16[4,256,128]{2,1,0:T(8,128)(2,1)S(1)}, u32[]{:S(2)}, u32[]{:S(2)}) collective-permute-start(bf16[4,256,128]{2,1,0:T(8,128)(2,1)S(1)} %get-tuple-element.59.kv0), channel_id=1, source_target_pairs={{0,48},{1,49},{2,50},{3,51},{4,52},{5,53},{6,54},{7,55},{8,24},{9,... | collective-permute-start | bytes 786440 | tf_op jit(solution)/shard_map/ppermute | solution.py:82
  26.2 0.7 copy-start.2
  26.9 0.7 copy-start.3
  30.6 2.4 %collective-permute-start.7 = (bf16[4,528,128]{2,1,0:T(8,128)(2,1)S(1)}, bf16[4,528,128]{2,1,0:T(8,128)(2,1)S(1)}, u32[]{:S(2)}, u32[]{:S(2)}) collective-permute-start(bf16[4,528,128]{2,1,0:T(8,128)(2,1)S(1)} %get-tuple-element.58.q0), channel_id=1, source_target_pairs={{0,8},{1,9},{2,10},{3,11},{4,12},{5,13},{6,14},{7,15},{8,0},{9,1},... | collective-permute-start | bytes 1622024 | tf_op jit(solution)/shard_map/ppermute | solution.py:82
  30.9 2.5 %collective-permute-start.8 = (bf16[4,528,128]{2,1,0:T(8,128)(2,1)S(1)}, bf16[4,528,128]{2,1,0:T(8,128)(2,1)S(1)}, u32[]{:S(2)}, u32[]{:S(2)}) collective-permute-start(bf16[4,528,128]{2,1,0:T(8,128)(2,1)S(1)} %collective-permute-done.4.q1), channel_id=1, source_target_pairs={{0,8},{1,9},{2,10},{3,11},{4,12},{5,13},{6,14},{7,15},{8,0},{9,1},... | collective-permute-start | bytes 1622024 | tf_op jit(solution)/shard_map/ppermute | solution.py:82
  31.3 7.6 %collective-permute-start.9 = (bf16[4,256,128]{2,1,0:T(8,128)(2,1)S(1)}, bf16[4,256,128]{2,1,0:T(8,128)(2,1)S(1)}, u32[]{:S(2)}, u32[]{:S(2)}) collective-permute-start(bf16[4,256,128]{2,1,0:T(8,128)(2,1)S(1)} %collective-permute-done.5.kv1), channel_id=1, source_target_pairs={{0,48},{1,49},{2,50},{3,51},{4,52},{5,53},{6,54},{7,55},{8,24},{9,... | collective-permute-start | bytes 786440 | tf_op jit(solution)/shard_map/ppermute | solution.py:82
  42.3 7.7 %collective-permute-start.11 = (bf16[4,256,128]{2,1,0:T(8,128)(2,1)S(1)}, bf16[4,256,128]{2,1,0:T(8,128)(2,1)S(1)}, u32[]{:S(2)}, u32[]{:S(2)}) collective-permute-start(bf16[4,256,128]{2,1,0:T(8,128)(2,1)S(1)} %get-tuple-element.75), channel_id=1, source_target_pairs={{0,48},{1,49},{2,50},{3,51},{4,52},{5,53},{6,54},{7,55},{8,24},{9,... | collective-permute-start | bytes 786440 | tf_op jit(solution)/shard_map/ppermute | solution.py:82
  47.6 1.4 %collective-permute-start.12 = (bf16[2,128,256]{2,1,0:T(8,128)(2,1)S(1)}, bf16[2,128,256]{2,1,0:T(8,128)(2,1)S(1)}, u32[]{:S(2)}, u32[]{:S(2)}) collective-permute-start(bf16[2,128,256]{2,1,0:T(8,128)(2,1)S(1)} %get-tuple-element.76), channel_id=1, source_target_pairs={{0,8},{1,9},{2,10},{3,11},{4,12},{5,13},{6,14},{7,15},{8,0},{9,1},... | collective-permute-start | bytes 393224 | tf_op jit(solution)/shard_map/ppermute | solution.py:82
  47.7 1.5 %collective-permute-start.13 = (bf16[2,128,256]{2,1,0:T(8,128)(2,1)S(1)}, bf16[2,128,256]{2,1,0:T(8,128)(2,1)S(1)}, u32[]{:S(2)}, u32[]{:S(2)}) collective-permute-start(bf16[2,128,256]{2,1,0:T(8,128)(2,1)S(1)} %get-tuple-element.77), channel_id=1, source_target_pairs={{0,8},{1,9},{2,10},{3,11},{4,12},{5,13},{6,14},{7,15},{8,0},{9,1},... | collective-permute-start | bytes 393224 | tf_op jit(solution)/shard_map/ppermute | solution.py:82
  48.2 1.3 %collective-permute-start.14 = (bf16[2,128,256]{2,1,0:T(8,128)(2,1)S(1)}, bf16[2,128,256]{2,1,0:T(8,128)(2,1)S(1)}, u32[]{:S(2)}, u32[]{:S(2)}) collective-permute-start(bf16[2,128,256]{2,1,0:T(8,128)(2,1)S(1)} %get-tuple-element.78), channel_id=1, source_target_pairs={{0,8},{1,9},{2,10},{3,11},{4,12},{5,13},{6,14},{7,15},{8,0},{9,1},... | collective-permute-start | bytes 393224 | tf_op jit(solution)/shard_map/ppermute | solution.py:82
  48.3 1.4 %collective-permute-start.15 = (bf16[2,128,256]{2,1,0:T(8,128)(2,1)S(1)}, bf16[2,128,256]{2,1,0:T(8,128)(2,1)S(1)}, u32[]{:S(2)}, u32[]{:S(2)}) collective-permute-start(bf16[2,128,256]{2,1,0:T(8,128)(2,1)S(1)} %get-tuple-element.79), channel_id=1, source_target_pairs={{0,8},{1,9},{2,10},{3,11},{4,12},{5,13},{6,14},{7,15},{8,0},{9,1},... | collective-permute-start | bytes 393224 | tf_op jit(solution)/shard_map/ppermute | solution.py:82
  49.1 10.1 %collective-permute-start.10 = (bf16[4,256,128]{2,1,0:T(8,128)(2,1)S(1)}, bf16[4,256,128]{2,1,0:T(8,128)(2,1)S(1)}, u32[]{:S(2)}, u32[]{:S(2)}) collective-permute-start(bf16[4,256,128]{2,1,0:T(8,128)(2,1)S(1)} %get-tuple-element.74), channel_id=1, source_target_pairs={{0,48},{1,49},{2,50},{3,51},{4,52},{5,53},{6,54},{7,55},{8,24},{9,... | collective-permute-start | bytes 786440 | tf_op jit(solution)/shard_map/ppermute | solution.py:82
  50.0 9.1 %collective-permute-start.17 = (bf16[4,128,256]{2,1,0:T(8,128)(2,1)S(1)}, bf16[4,128,256]{2,1,0:T(8,128)(2,1)S(1)}, u32[]{:S(2)}, u32[]{:S(2)}) collective-permute-start(bf16[4,128,256]{2,1,0:T(8,128)(2,1)S(1)} %add_convert_fusion), channel_id=1, source_target_pairs={{0,3},{1,2},{2,1},{3,0},{4,7},{5,6},{6,5},{7,4},{8,9},{9,8},{10,11... | collective-permute-start | bytes 786440 | tf_op jit(solution)/shard_map/ppermute | solution.py:82
  50.2 9.0 %collective-permute-start.16 = (bf16[4,256,128]{2,1,0:T(8,128)(2,1)S(1)}, bf16[4,256,128]{2,1,0:T(8,128)(2,1)S(1)}, u32[]{:S(2)}, u32[]{:S(2)}) collective-permute-start(bf16[4,256,128]{2,1,0:T(8,128)(2,1)S(1)} %add_convert_fusion.1), channel_id=1, source_target_pairs={{0,16},{1,17},{2,18},{3,19},{4,20},{5,21},{6,22},{7,23},{8,56},{9,... | collective-permute-start | bytes 786440 | tf_op jit(solution)/shard_map/ppermute | solution.py:82
  59.3 7.3 %collective-permute-start.21 = (bf16[2,128,256]{2,1,0:T(8,128)(2,1)S(1)}, bf16[2,128,256]{2,1,0:T(8,128)(2,1)S(1)}, u32[]{:S(2)}, u32[]{:S(2)}) collective-permute-start(bf16[2,128,256]{2,1,0:T(8,128)(2,1)S(1)} %slice.58), channel_id=1, source_target_pairs={{0,1},{1,0},{2,3},{3,2},{4,5},{5,4},{6,7},{7,6},{8,11},{9,10},{10,... | collective-permute-start | bytes 393224 | tf_op jit(solution)/shard_map/ppermute | solution.py:82
  60.7 10.1 %collective-permute-start.18 = (bf16[1,256,128]{2,1,0:T(8,128)(2,1)S(1)}, bf16[1,256,128]{2,1,0:T(8,128)(2,1)S(1)}, u32[]{:S(2)}, u32[]{:S(2)}) collective-permute-start(bf16[1,256,128]{2,1,0:T(8,128)(2,1)S(1)} %get-tuple-element.93), channel_id=1, source_target_pairs={{0,192},{1,193},{2,194},{3,195},{4,196},{5,197},{6,198},{7,199},{8... | collective-permute-start | bytes 196616 | tf_op jit(solution)/shard_map/ppermute | solution.py:82
  65.9 4.9 %collective-permute-start.19 = (bf16[1,256,128]{2,1,0:T(8,128)(2,1)S(1)}, bf16[1,256,128]{2,1,0:T(8,128)(2,1)S(1)}, u32[]{:S(2)}, u32[]{:S(2)}) collective-permute-start(bf16[1,256,128]{2,1,0:T(8,128)(2,1)S(1)} %get-tuple-element.92), channel_id=1, source_target_pairs={{0,4},{1,5},{2,6},{3,7},{4,0},{5,1},{6,2},{7,3},{8,12},{9,13},{10,... | collective-permute-start | bytes 196616 | tf_op jit(solution)/shard_map/ppermute | solution.py:82
  65.9 5.5 %collective-permute-start.20 = (bf16[1,256,128]{2,1,0:T(8,128)(2,1)S(1)}, bf16[1,256,128]{2,1,0:T(8,128)(2,1)S(1)}, u32[]{:S(2)}, u32[]{:S(2)}) collective-permute-start(bf16[1,256,128]{2,1,0:T(8,128)(2,1)S(1)} %get-tuple-element.91), channel_id=1, source_target_pairs={{0,196},{1,197},{2,198},{3,199},{4,192},{5,193},{6,194},{7,195},{8... | collective-permute-start | bytes 196616 | tf_op jit(solution)/shard_map/ppermute | solution.py:82
  66.6 6.7 %collective-permute-start.22 = (bf16[1,128,256]{2,1,0:T(8,128)(2,1)S(1)}, bf16[1,128,256]{2,1,0:T(8,128)(2,1)S(1)}, u32[]{:S(2)}, u32[]{:S(2)}) collective-permute-start(bf16[1,128,256]{2,1,0:T(8,128)(2,1)S(1)} %slice.59), channel_id=1, source_target_pairs={{0,64},{1,65},{2,66},{3,67},{4,68},{5,69},{6,70},{7,71},{8,72},{9,... | collective-permute-start | bytes 196616 | tf_op jit(solution)/shard_map/ppermute | solution.py:82
where the time goes:
time: 74.4 us; the launch traced here: 74.1 us
  starting transfers between devices  32 us (43%)
  waiting for transfers between devices  20.4 us (27%)
  Pallas kernels  16.8 us (23%)
  local copies, waits for them, and re-layouts  3.81 us (5%)
  between operations  0.78 us (1%)
    ppermute x23, starting transfers between devices, swap(): return lax.ppermute(value, AXES, [(i, int(to[i])) for i in range(256)])  32 us
    ppermute x23, waiting for transfers between devices, swap(): return lax.ppermute(value, AXES, [(i, int(to[i])) for i in range(256)])  20.4 us
    pallas_call x3, Pallas kernels, compute(): pl.pallas_call(kernel, out_shape=outs, in_specs=[spec(pltpu.SMEM)] * 2 +...  11.1 us
    pallas_call x1, Pallas kernels, body(): pl.pallas_call(list_kernel, out_shape=(jax.ShapeDtypeStruct((LISTS + 3 *...  3.12 us
    unnamed x8, local copies, waits for them, and re-layouts  3.08 us
    pallas_call x1, Pallas kernels, body(): pl.pallas_call(prep_kernel, out_shape=(jax.ShapeDtypeStruct((1, QROWS, TO...  1.7 us
  transfers between devices with their start and end apart: 23, of which 14 were waited for; matrix products, arithmetic and copies ran while one was open for 1% of the time, Pallas kernels for 15%

commit v1 on v0

--- a/solution.py
+++ b/solution.py
@@ -15,7 +15,7 @@
 HALF = GROUP // 2
 PARTS = ((0, 8), (12, 16), (8, 12))
 LISTS, LIST = 8, GROUP * HALF // 2 + 8
-UNROLL = (2, 2, 2)
+UNROLL = (3, 3, 3)
 
 
 def coords(i):

time: 74.4 us -> 74.9 us (level); the launches traced: 74.1 us -> 75.6 us
  waiting for transfers between devices: 20.4 us -> 23.1 us
  Pallas kernels: 16.8 us -> 14.9 us
    ppermute x23, waiting for transfers between devices: 20.4 us -> 23.1 us  [swap(): return lax.ppermute(value, AXES, [(i, int(to[i])) for i in range(256)])]
    pallas_call x3, Pallas kernels: 11.1 us -> 9.23 us  [compute(): pl.pallas_call(kernel, out_shape=outs, in_specs=[spec(pltpu.SMEM)] * 2 +...]
  transfers between devices with their start and end apart: 23 -> 23, of which waited for: 14 -> 13; matrix products, arithmetic and copies ran while one was open for 1% -> 1% of each run, Pallas kernels for 15% -> 12%
where the time goes in v1:
time: 74.9 us; the launch traced here: 75.6 us
  starting transfers between devices  32.6 us (44%)
  waiting for transfers between devices  23.1 us (31%)
  Pallas kernels  14.9 us (20%)
  local copies, waits for them, and re-layouts  3.81 us (5%)
  between operations  0.81 us (1%)
    ppermute x23, starting transfers between devices, swap(): return lax.ppermute(value, AXES, [(i, int(to[i])) for i in range(256)])  32.6 us
    ppermute x23, waiting for transfers between devices, swap(): return lax.ppermute(value, AXES, [(i, int(to[i])) for i in range(256)])  23.1 us
    pallas_call x3, Pallas kernels, compute(): pl.pallas_call(kernel, out_shape=outs, in_specs=[spec(pltpu.SMEM)] * 2 +...  9.23 us
    pallas_call x1, Pallas kernels, body(): pl.pallas_call(list_kernel, out_shape=(jax.ShapeDtypeStruct((LISTS + 3 *...  3.13 us
    unnamed x8, local copies, waits for them, and re-layouts  3.08 us
    pallas_call x1, Pallas kernels, body(): pl.pallas_call(prep_kernel, out_shape=(jax.ShapeDtypeStruct((1, QROWS, TO...  1.7 us
  transfers between devices with their start and end apart: 23, of which 13 were waited for; matrix products, arithmetic and copies ran while one was open for 1% of the time, Pallas kernels for 12%

profile of v1, /device:TPU:2, one launch (start us, length us, event | category | flops | bytes accessed | tf_op | source)
XLA Modules:
  0.0 75.6 jit_solution(14232675298014109830)
XLA Ops:
  0.6 1.7 %prep.1 = (bf16[1,528,128]{2,1,0:T(8,128)(2,1)}, bf16[1,256,128]{2,1,0:T(8,128)(2,1)}) custom-call(bf16[128,256]{1,0:T(8,128)(2,1)} %q_ref.1, bf16[128,256]{1,0:T(8,128)(2,1)} %g_ref.1, bf16[128,256]{1,0:T(8,128)(2,1)} %o_ref.1, f32[2,128]{1,0:T(2,128)} %n_ref.1, bf16[128,128]{1,0:T(8,128)(2,1)} %k_ref.1, bf16[128,128]{1,0:T(8,128)(2,1)} %v_ref.1), custom_call_target="tpu_custom_call" | custom-call | tf_op jit(solution)/shard_map/prep/pallas_call | solution.py:269
  2.3 3.3 %collective-permute-start = (bf16[1,528,128]{2,1,0:T(8,128)(2,1)}, bf16[1,528,128]{2,1,0:T(8,128)(2,1)S(1)}, u32[]{:S(2)}, u32[]{:S(2)}) collective-permute-start(bf16[1,528,128]{2,1,0:T(8,128)(2,1)} %get-tuple-element.46.a0), channel_id=1, source_target_pairs={{0,64},{1,65},{2,66},{3,67},{4,68},{5,69},{6,70},{7,71},{8,72},{9,... | collective-permute-start | bytes 405512 | tf_op jit(solution)/shard_map/ppermute | solution.py:82
  5.6 4.5 %collective-permute-start.1 = (bf16[1,256,128]{2,1,0:T(8,128)(2,1)}, bf16[1,256,128]{2,1,0:T(8,128)(2,1)S(1)}, u32[]{:S(2)}, u32[]{:S(2)}) collective-permute-start(bf16[1,256,128]{2,1,0:T(8,128)(2,1)} %get-tuple-element.47.b0), channel_id=1, source_target_pairs={{0,192},{1,193},{2,194},{3,195},{4,196},{5,197},{6,198},{7,199},{8... | collective-permute-start | bytes 196616 | tf_op jit(solution)/shard_map/ppermute | solution.py:82
  10.1 0.9 %copy-done = bf16[1,528,128]{2,1,0:T(8,128)(2,1)S(1)} copy-done((bf16[1,528,128]{2,1,0:T(8,128)(2,1)S(1)}, bf16[1,528,128]{2,1,0:T(8,128)(2,1)}, u32[]{:S(2)}) %copy-start) | copy-done | bytes 135192
  11.0 0.8 %copy-done.1 = bf16[1,256,128]{2,1,0:T(8,128)(2,1)S(1)} copy-done((bf16[1,256,128]{2,1,0:T(8,128)(2,1)S(1)}, bf16[1,256,128]{2,1,0:T(8,128)(2,1)}, u32[]{:S(2)}) %copy-start.1) | copy-done | bytes 65560
  11.8 1.7 %collective-permute-done.1.b1 = bf16[1,256,128]{2,1,0:T(8,128)(2,1)S(1)} collective-permute-done((bf16[1,256,128]{2,1,0:T(8,128)(2,1)}, bf16[1,256,128]{2,1,0:T(8,128)(2,1)S(1)}, u32[]{:S(2)}, u32[]{:S(2)}) %collective-permute-start.1) | collective-permute-done | bytes 65568 | tf_op jit(solution)/shard_map/ppermute | solution.py:82
  13.6 0.6 collective-permute-start.2
  14.2 1.3 %collective-permute-start.3 = (bf16[2,256,128]{2,1,0:T(8,128)(2,1)S(1)}, bf16[2,256,128]{2,1,0:T(8,128)(2,1)S(1)}, u32[]{:S(2)}, u32[]{:S(2)}) collective-permute-start(bf16[2,256,128]{2,1,0:T(8,128)(2,1)S(1)} %get-tuple-element.55.b0), channel_id=1, source_target_pairs={{0,4},{1,5},{2,6},{3,7},{4,0},{5,1},{6,2},{7,3},{8,12},{9,13},{10,... | collective-permute-start | bytes 393224 | tf_op jit(solution)/shard_map/ppermute | solution.py:82
  15.5 3.7 %collective-permute-done.3.b1 = bf16[2,256,128]{2,1,0:T(8,128)(2,1)S(1)} collective-permute-done((bf16[2,256,128]{2,1,0:T(8,128)(2,1)S(1)}, bf16[2,256,128]{2,1,0:T(8,128)(2,1)S(1)}, u32[]{:S(2)}, u32[]{:S(2)}) %collective-permute-start.3) | collective-permute-done | bytes 131104 | tf_op jit(solution)/shard_map/ppermute | solution.py:82
  19.1 1.0 %collective-permute-done.2.a1 = bf16[2,528,128]{2,1,0:T(8,128)(2,1)S(1)} collective-permute-done((bf16[2,528,128]{2,1,0:T(8,128)(2,1)S(1)}, bf16[2,528,128]{2,1,0:T(8,128)(2,1)S(1)}, u32[]{:S(2)}, u32[]{:S(2)}) %collective-permute-start.2) | collective-permute-done | bytes 270368 | tf_op jit(solution)/shard_map/ppermute | solution.py:82
  20.2 1.6 %collective-permute-start.4 = (bf16[4,528,128]{2,1,0:T(8,128)(2,1)S(1)}, bf16[4,528,128]{2,1,0:T(8,128)(2,1)S(1)}, u32[]{:S(2)}, u32[]{:S(2)}) collective-permute-start(bf16[4,528,128]{2,1,0:T(8,128)(2,1)S(1)} %get-tuple-element.58.q0), channel_id=1, source_target_pairs={{0,3},{1,2},{2,1},{3,0},{4,7},{5,6},{6,5},{7,4},{8,9},{9,8},{10,11... | collective-permute-start | bytes 1622024 | tf_op jit(solution)/shard_map/ppermute | solution.py:82
  21.7 1.6 %collective-permute-start.5 = (bf16[4,256,128]{2,1,0:T(8,128)(2,1)S(1)}, bf16[4,256,128]{2,1,0:T(8,128)(2,1)S(1)}, u32[]{:S(2)}, u32[]{:S(2)}) collective-permute-start(bf16[4,256,128]{2,1,0:T(8,128)(2,1)S(1)} %get-tuple-element.59.kv0), channel_id=1, source_target_pairs={{0,16},{1,17},{2,18},{3,19},{4,20},{5,21},{6,22},{7,23},{8,56},{9,... | collective-permute-start | bytes 786440 | tf_op jit(solution)/shard_map/ppermute | solution.py:82
  23.3 2.2 %collective-permute-start.6 = (bf16[4,256,128]{2,1,0:T(8,128)(2,1)S(1)}, bf16[4,256,128]{2,1,0:T(8,128)(2,1)S(1)}, u32[]{:S(2)}, u32[]{:S(2)}) collective-permute-start(bf16[4,256,128]{2,1,0:T(8,128)(2,1)S(1)} %get-tuple-element.59.kv0), channel_id=1, source_target_pairs={{0,48},{1,49},{2,50},{3,51},{4,52},{5,53},{6,54},{7,55},{8,24},{9,... | collective-permute-start | bytes 786440 | tf_op jit(solution)/shard_map/ppermute | solution.py:82
  25.5 0.7 dynamic-slice_bitcast_fusion.ids_ref
  26.2 0.7 copy-done.2
  26.9 0.7 copy-done.3
  27.5 3.1 %tiles.1 = (s32[224]{0:T(256)S(1)}, s32[64]{0:T(128)S(1)}, s32[16,8,128]{2,1,0:T(8,128)S(1)}) custom-call(s32[256]{0:T(256)S(1)} %copy-done.2, s32[16]{0:T(128)S(1)} %copy-done.3, s32[32]{0:T(128)S(1)} %dynamic-slice_bitcast_fusion.ids_ref), custom_call_target="tpu_custom_call" | custom-call | tf_op jit(solution)/shard_map/tiles/pallas_call | solution.py:281
  31.3 1.7 %collective-permute-start.9 = (bf16[4,256,128]{2,1,0:T(8,128)(2,1)S(1)}, bf16[4,256,128]{2,1,0:T(8,128)(2,1)S(1)}, u32[]{:S(2)}, u32[]{:S(2)}) collective-permute-start(bf16[4,256,128]{2,1,0:T(8,128)(2,1)S(1)} %collective-permute-done.5.kv1), channel_id=1, source_target_pairs={{0,48},{1,49},{2,50},{3,51},{4,52},{5,53},{6,54},{7,55},{8,24},{9,... | collective-permute-start | bytes 786440 | tf_op jit(solution)/shard_map/ppermute | solution.py:82
  33.4 2.9 %first.1 = (bf16[16,528,128]{2,1,0:T(8,128)(2,1)S(1)}, f32[16,8,256]{2,1,0:T(8,128)S(1)}, f32[16,128,256]{2,1,0:T(8,128)S(1)}, f32[8,256,128]{2,1,0:T(8,128)S(1)}) custom-call(s32[224]{0:T(256)S(1)} %get-tuple-element.63.list_ref, s32[64]{0:T(128)S(1)} %get-tuple-element.64.base_ref, s32[16,8,128]{2,1,0:T(8,128)S(1)} %get-tuple-element.65.rows_ref, ...), custom_call_target="tpu_custom_call" | custom-call | flops 3000000000 | bytes 10000000 | tf_op jit(solution)/shard_map/first/pallas_call | solution.py:311
  36.3 2.6 %collective-permute-done.9.kv_ref = bf16[4,256,128]{2,1,0:T(8,128)(2,1)S(1)} collective-permute-done((bf16[4,256,128]{2,1,0:T(8,128)(2,1)S(1)}, bf16[4,256,128]{2,1,0:T(8,128)(2,1)S(1)}, u32[]{:S(2)}, u32[]{:S(2)}) %collective-permute-start.9) | collective-permute-done | bytes 262176 | tf_op jit(solution)/shard_map/ppermute | solution.py:82
  38.9 3.6 %far.1 = (f32[16,128,256]{2,1,0:T(8,128)S(1)}, bf16[4,256,128]{2,1,0:T(8,128)(2,1)S(1)}) custom-call(s32[224]{0:T(256)S(1)} %get-tuple-element.63.list_ref, s32[64]{0:T(128)S(1)} %get-tuple-element.64.base_ref, s32[16,8,128]{2,1,0:T(8,128)S(1)} %get-tuple-element.65.rows_ref, bf16[16,528,128]{2,1,0:T(8,128)(2,1)S(1)} %get-tuple-element.69.q_all, ...), custom_call_target="tpu_custom_call" | custom-call | flops 3000000000 | bytes 10000000 | tf_op jit(solution)/shard_map/far/pallas_call | solution.py:311
  42.6 2.8 %last.1 = (f32[8,128,256]{2,1,0:T(8,128)S(1)}, bf16[2,128,256]{2,1,0:T(8,128)(2,1)S(1)}, bf16[2,128,256]{2,1,0:T(8,128)(2,1)S(1)}, bf16[2,128,256]{2,1,0:T(8,128...) custom-call(s32[224]{0:T(256)S(1)} %get-tuple-element.63.list_ref, ...), custom_call_target="tpu_custom_call" | custom-call | flops 3000000000 | bytes 10000000 | tf_op jit(solution)/shard_map/last/pallas_call | solution.py:311
  46.8 2.3 %collective-permute-start.10 = (bf16[4,256,128]{2,1,0:T(8,128)(2,1)S(1)}, bf16[4,256,128]{2,1,0:T(8,128)(2,1)S(1)}, u32[]{:S(2)}, u32[]{:S(2)}) collective-permute-start(bf16[4,256,128]{2,1,0:T(8,128)(2,1)S(1)} %get-tuple-element.74), channel_id=1, source_target_pairs={{0,48},{1,49},{2,50},{3,51},{4,52},{5,53},{6,54},{7,55},{8,24},{9,... | collective-permute-start | bytes 786440 | tf_op jit(solution)/shard_map/ppermute | solution.py:82
  49.1 1.0 %collective-permute-done.11 = bf16[4,256,128]{2,1,0:T(8,128)(2,1)S(1)} collective-permute-done((bf16[4,256,128]{2,1,0:T(8,128)(2,1)S(1)}, bf16[4,256,128]{2,1,0:T(8,128)(2,1)S(1)}, u32[]{:S(2)}, u32[]{:S(2)}) %collective-permute-start.11) | collective-permute-done | bytes 262176 | tf_op jit(solution)/shard_map/ppermute | solution.py:82
  50.5 4.8 %collective-permute-done.10 = bf16[4,256,128]{2,1,0:T(8,128)(2,1)S(1)} collective-permute-done((bf16[4,256,128]{2,1,0:T(8,128)(2,1)S(1)}, bf16[4,256,128]{2,1,0:T(8,128)(2,1)S(1)}, u32[]{:S(2)}, u32[]{:S(2)}) %collective-permute-start.10) | collective-permute-done | bytes 262176 | tf_op jit(solution)/shard_map/ppermute | solution.py:82
  55.3 1.4 %collective-permute-done.17 = bf16[4,128,256]{2,1,0:T(8,128)(2,1)S(1)} collective-permute-done((bf16[4,128,256]{2,1,0:T(8,128)(2,1)S(1)}, bf16[4,128,256]{2,1,0:T(8,128)(2,1)S(1)}, u32[]{:S(2)}, u32[]{:S(2)}) %collective-permute-start.17) | collective-permute-done | bytes 262176 | tf_op jit(solution)/shard_map/ppermute | solution.py:82
  57.0 3.7 %collective-permute-start.21 = (bf16[2,128,256]{2,1,0:T(8,128)(2,1)S(1)}, bf16[2,128,256]{2,1,0:T(8,128)(2,1)S(1)}, u32[]{:S(2)}, u32[]{:S(2)}) collective-permute-start(bf16[2,128,256]{2,1,0:T(8,128)(2,1)S(1)} %slice.58), channel_id=1, source_target_pairs={{0,1},{1,0},{2,3},{3,2},{4,5},{5,4},{6,7},{7,6},{8,11},{9,10},{10,... | collective-permute-start | bytes 393224 | tf_op jit(solution)/shard_map/ppermute | solution.py:82
  60.9 5.4 %collective-permute-start.18 = (bf16[1,256,128]{2,1,0:T(8,128)(2,1)S(1)}, bf16[1,256,128]{2,1,0:T(8,128)(2,1)S(1)}, u32[]{:S(2)}, u32[]{:S(2)}) collective-permute-start(bf16[1,256,128]{2,1,0:T(8,128)(2,1)S(1)} %get-tuple-element.93), channel_id=1, source_target_pairs={{0,192},{1,193},{2,194},{3,195},{4,196},{5,197},{6,198},{7,199},{8... | collective-permute-start | bytes 196616 | tf_op jit(solution)/shard_map/ppermute | solution.py:82
  66.2 2.4 %collective-permute-start.19 = (bf16[1,256,128]{2,1,0:T(8,128)(2,1)S(1)}, bf16[1,256,128]{2,1,0:T(8,128)(2,1)S(1)}, u32[]{:S(2)}, u32[]{:S(2)}) collective-permute-start(bf16[1,256,128]{2,1,0:T(8,128)(2,1)S(1)} %get-tuple-element.92), channel_id=1, source_target_pairs={{0,4},{1,5},{2,6},{3,7},{4,0},{5,1},{6,2},{7,3},{8,12},{9,13},{10,... | collective-permute-start | bytes 196616 | tf_op jit(solution)/shard_map/ppermute | solution.py:82
  68.8 2.8 %collective-permute-done.19.g2 = bf16[1,256,128]{2,1,0:T(8,128)(2,1)S(1)} collective-permute-done((bf16[1,256,128]{2,1,0:T(8,128)(2,1)S(1)}, bf16[1,256,128]{2,1,0:T(8,128)(2,1)S(1)}, u32[]{:S(2)}, u32[]{:S(2)}) %collective-permute-start.19) | collective-permute-done | bytes 65568 | tf_op jit(solution)/shard_map/ppermute | solution.py:82
  71.6 3.2 %collective-permute-done.20.g3 = bf16[1,256,128]{2,1,0:T(8,128)(2,1)S(1)} collective-permute-done((bf16[1,256,128]{2,1,0:T(8,128)(2,1)S(1)}, bf16[1,256,128]{2,1,0:T(8,128)(2,1)S(1)}, u32[]{:S(2)}, u32[]{:S(2)}) %collective-permute-start.20) | collective-permute-done | bytes 65568 | tf_op jit(solution)/shard_map/ppermute | solution.py:82
  74.8 0.8 %finish.1 = (f32[128,256]{1,0:T(8,128)}, f32[128,128]{1,0:T(8,128)}, f32[128,128]{1,0:T(8,128)}) custom-call(f32[4,256,128]{2,1,0:T(8,128)S(1)} %get-tuple-element.90.g_ref, bf16[1,256,128]{2,1,0:T(8,128)(2,1)S(1)} %collective-permute-done.18.g1, bf16[1,256,128]{2,1,0:T(8,128)(2,1)S(1)} %collective-permute-done.19.g2, ...), custom_call_target="tpu_custom_call" | custom-call | tf_op jit(solution)/shard_map/finish/pallas_call | solution.py:383
  (40 shorter events, 3.5 us)
Async XLA Ops:
  2.3 11.2 %collective-permute-start = (bf16[1,528,128]{2,1,0:T(8,128)(2,1)}, bf16[1,528,128]{2,1,0:T(8,128)(2,1)S(1)}, u32[]{:S(2)}, u32[]{:S(2)}) collective-permute-start(bf16[1,528,128]{2,1,0:T(8,128)(2,1)} %get-tuple-element.46.a0), channel_id=1, source_target_pairs={{0,64},{1,65},{2,66},{3,67},{4,68},{5,69},{6,70},{7,71},{8,72},{9,... | collective-permute-start | bytes 405512 | tf_op jit(solution)/shard_map/ppermute | solution.py:82
  5.6 7.9 %collective-permute-start.1 = (bf16[1,256,128]{2,1,0:T(8,128)(2,1)}, bf16[1,256,128]{2,1,0:T(8,128)(2,1)S(1)}, u32[]{:S(2)}, u32[]{:S(2)}) collective-permute-start(bf16[1,256,128]{2,1,0:T(8,128)(2,1)} %get-tuple-element.47.b0), channel_id=1, source_target_pairs={{0,192},{1,193},{2,194},{3,195},{4,196},{5,197},{6,198},{7,199},{8... | collective-permute-start | bytes 196616 | tf_op jit(solution)/shard_map/ppermute | solution.py:82
  10.1 0.9 %copy-start = (bf16[1,528,128]{2,1,0:T(8,128)(2,1)S(1)}, bf16[1,528,128]{2,1,0:T(8,128)(2,1)}, u32[]{:S(2)}) copy-start(bf16[1,528,128]{2,1,0:T(8,128)(2,1)} %get-tuple-element.46.a0) | copy-start | bytes 405508
  11.0 0.8 %copy-start.1 = (bf16[1,256,128]{2,1,0:T(8,128)(2,1)S(1)}, bf16[1,256,128]{2,1,0:T(8,128)(2,1)}, u32[]{:S(2)}) copy-start(bf16[1,256,128]{2,1,0:T(8,128)(2,1)} %get-tuple-element.47.b0) | copy-start | bytes 196612
  13.6 6.5 %collective-permute-start.2 = (bf16[2,528,128]{2,1,0:T(8,128)(2,1)S(1)}, bf16[2,528,128]{2,1,0:T(8,128)(2,1)S(1)}, u32[]{:S(2)}, u32[]{:S(2)}) collective-permute-start(bf16[2,528,128]{2,1,0:T(8,128)(2,1)S(1)} %get-tuple-element.54.a0), channel_id=1, source_target_pairs={{0,1},{1,0},{2,3},{3,2},{4,5},{5,4},{6,7},{7,6},{8,11},{9,10},{10,... | collective-permute-start | bytes 811016 | tf_op jit(solution)/shard_map/ppermute | solution.py:82
  14.2 5.0 %collective-permute-start.3 = (bf16[2,256,128]{2,1,0:T(8,128)(2,1)S(1)}, bf16[2,256,128]{2,1,0:T(8,128)(2,1)S(1)}, u32[]{:S(2)}, u32[]{:S(2)}) collective-permute-start(bf16[2,256,128]{2,1,0:T(8,128)(2,1)S(1)} %get-tuple-element.55.b0), channel_id=1, source_target_pairs={{0,4},{1,5},{2,6},{3,7},{4,0},{5,1},{6,2},{7,3},{8,12},{9,13},{10,... | collective-permute-start | bytes 393224 | tf_op jit(solution)/shard_map/ppermute | solution.py:82
  20.2 10.7 %collective-permute-start.4 = (bf16[4,528,128]{2,1,0:T(8,128)(2,1)S(1)}, bf16[4,528,128]{2,1,0:T(8,128)(2,1)S(1)}, u32[]{:S(2)}, u32[]{:S(2)}) collective-permute-start(bf16[4,528,128]{2,1,0:T(8,128)(2,1)S(1)} %get-tuple-element.58.q0), channel_id=1, source_target_pairs={{0,3},{1,2},{2,1},{3,0},{4,7},{5,6},{6,5},{7,4},{8,9},{9,8},{10,11... | collective-permute-start | bytes 1622024 | tf_op jit(solution)/shard_map/ppermute | solution.py:82
  21.7 9.0 %collective-permute-start.5 = (bf16[4,256,128]{2,1,0:T(8,128)(2,1)S(1)}, bf16[4,256,128]{2,1,0:T(8,128)(2,1)S(1)}, u32[]{:S(2)}, u32[]{:S(2)}) collective-permute-start(bf16[4,256,128]{2,1,0:T(8,128)(2,1)S(1)} %get-tuple-element.59.kv0), channel_id=1, source_target_pairs={{0,16},{1,17},{2,18},{3,19},{4,20},{5,21},{6,22},{7,23},{8,56},{9,... | collective-permute-start | bytes 786440 | tf_op jit(solution)/shard_map/ppermute | solution.py:82
  23.3 7.6 %collective-permute-start.6 = (bf16[4,256,128]{2,1,0:T(8,128)(2,1)S(1)}, bf16[4,256,128]{2,1,0:T(8,128)(2,1)S(1)}, u32[]{:S(2)}, u32[]{:S(2)}) collective-permute-start(bf16[4,256,128]{2,1,0:T(8,128)(2,1)S(1)} %get-tuple-element.59.kv0), channel_id=1, source_target_pairs={{0,48},{1,49},{2,50},{3,51},{4,52},{5,53},{6,54},{7,55},{8,24},{9,... | collective-permute-start | bytes 786440 | tf_op jit(solution)/shard_map/ppermute | solution.py:82
  26.2 0.7 copy-start.2
  26.9 0.7 copy-start.3
  30.7 2.4 %collective-permute-start.7 = (bf16[4,528,128]{2,1,0:T(8,128)(2,1)S(1)}, bf16[4,528,128]{2,1,0:T(8,128)(2,1)S(1)}, u32[]{:S(2)}, u32[]{:S(2)}) collective-permute-start(bf16[4,528,128]{2,1,0:T(8,128)(2,1)S(1)} %get-tuple-element.58.q0), channel_id=1, source_target_pairs={{0,8},{1,9},{2,10},{3,11},{4,12},{5,13},{6,14},{7,15},{8,0},{9,1},... | collective-permute-start | bytes 1622024 | tf_op jit(solution)/shard_map/ppermute | solution.py:82
  30.9 2.6 %collective-permute-start.8 = (bf16[4,528,128]{2,1,0:T(8,128)(2,1)S(1)}, bf16[4,528,128]{2,1,0:T(8,128)(2,1)S(1)}, u32[]{:S(2)}, u32[]{:S(2)}) collective-permute-start(bf16[4,528,128]{2,1,0:T(8,128)(2,1)S(1)} %collective-permute-done.4.q1), channel_id=1, source_target_pairs={{0,8},{1,9},{2,10},{3,11},{4,12},{5,13},{6,14},{7,15},{8,0},{9,1},... | collective-permute-start | bytes 1622024 | tf_op jit(solution)/shard_map/ppermute | solution.py:82
  31.3 7.6 %collective-permute-start.9 = (bf16[4,256,128]{2,1,0:T(8,128)(2,1)S(1)}, bf16[4,256,128]{2,1,0:T(8,128)(2,1)S(1)}, u32[]{:S(2)}, u32[]{:S(2)}) collective-permute-start(bf16[4,256,128]{2,1,0:T(8,128)(2,1)S(1)} %collective-permute-done.5.kv1), channel_id=1, source_target_pairs={{0,48},{1,49},{2,50},{3,51},{4,52},{5,53},{6,54},{7,55},{8,24},{9,... | collective-permute-start | bytes 786440 | tf_op jit(solution)/shard_map/ppermute | solution.py:82
  42.5 7.7 %collective-permute-start.11 = (bf16[4,256,128]{2,1,0:T(8,128)(2,1)S(1)}, bf16[4,256,128]{2,1,0:T(8,128)(2,1)S(1)}, u32[]{:S(2)}, u32[]{:S(2)}) collective-permute-start(bf16[4,256,128]{2,1,0:T(8,128)(2,1)S(1)} %get-tuple-element.75), channel_id=1, source_target_pairs={{0,48},{1,49},{2,50},{3,51},{4,52},{5,53},{6,54},{7,55},{8,24},{9,... | collective-permute-start | bytes 786440 | tf_op jit(solution)/shard_map/ppermute | solution.py:82
  45.4 1.4 %collective-permute-start.12 = (bf16[2,128,256]{2,1,0:T(8,128)(2,1)S(1)}, bf16[2,128,256]{2,1,0:T(8,128)(2,1)S(1)}, u32[]{:S(2)}, u32[]{:S(2)}) collective-permute-start(bf16[2,128,256]{2,1,0:T(8,128)(2,1)S(1)} %get-tuple-element.76), channel_id=1, source_target_pairs={{0,8},{1,9},{2,10},{3,11},{4,12},{5,13},{6,14},{7,15},{8,0},{9,1},... | collective-permute-start | bytes 393224 | tf_op jit(solution)/shard_map/ppermute | solution.py:82
  45.5 3.6 %collective-permute-start.13 = (bf16[2,128,256]{2,1,0:T(8,128)(2,1)S(1)}, bf16[2,128,256]{2,1,0:T(8,128)(2,1)S(1)}, u32[]{:S(2)}, u32[]{:S(2)}) collective-permute-start(bf16[2,128,256]{2,1,0:T(8,128)(2,1)S(1)} %get-tuple-element.77), channel_id=1, source_target_pairs={{0,8},{1,9},{2,10},{3,11},{4,12},{5,13},{6,14},{7,15},{8,0},{9,1},... | collective-permute-start | bytes 393224 | tf_op jit(solution)/shard_map/ppermute | solution.py:82
  46.0 3.1 %collective-permute-start.14 = (bf16[2,128,256]{2,1,0:T(8,128)(2,1)S(1)}, bf16[2,128,256]{2,1,0:T(8,128)(2,1)S(1)}, u32[]{:S(2)}, u32[]{:S(2)}) collective-permute-start(bf16[2,128,256]{2,1,0:T(8,128)(2,1)S(1)} %get-tuple-element.78), channel_id=1, source_target_pairs={{0,8},{1,9},{2,10},{3,11},{4,12},{5,13},{6,14},{7,15},{8,0},{9,1},... | collective-permute-start | bytes 393224 | tf_op jit(solution)/shard_map/ppermute | solution.py:82
  46.1 3.0 %collective-permute-start.15 = (bf16[2,128,256]{2,1,0:T(8,128)(2,1)S(1)}, bf16[2,128,256]{2,1,0:T(8,128)(2,1)S(1)}, u32[]{:S(2)}, u32[]{:S(2)}) collective-permute-start(bf16[2,128,256]{2,1,0:T(8,128)(2,1)S(1)} %get-tuple-element.79), channel_id=1, source_target_pairs={{0,8},{1,9},{2,10},{3,11},{4,12},{5,13},{6,14},{7,15},{8,0},{9,1},... | collective-permute-start | bytes 393224 | tf_op jit(solution)/shard_map/ppermute | solution.py:82
  46.8 8.5 %collective-permute-start.10 = (bf16[4,256,128]{2,1,0:T(8,128)(2,1)S(1)}, bf16[4,256,128]{2,1,0:T(8,128)(2,1)S(1)}, u32[]{:S(2)}, u32[]{:S(2)}) collective-permute-start(bf16[4,256,128]{2,1,0:T(8,128)(2,1)S(1)} %get-tuple-element.74), channel_id=1, source_target_pairs={{0,48},{1,49},{2,50},{3,51},{4,52},{5,53},{6,54},{7,55},{8,24},{9,... | collective-permute-start | bytes 786440 | tf_op jit(solution)/shard_map/ppermute | solution.py:82
  50.2 6.5 %collective-permute-start.17 = (bf16[4,128,256]{2,1,0:T(8,128)(2,1)S(1)}, bf16[4,128,256]{2,1,0:T(8,128)(2,1)S(1)}, u32[]{:S(2)}, u32[]{:S(2)}) collective-permute-start(bf16[4,128,256]{2,1,0:T(8,128)(2,1)S(1)} %add_convert_fusion), channel_id=1, source_target_pairs={{0,3},{1,2},{2,1},{3,0},{4,7},{5,6},{6,5},{7,4},{8,9},{9,8},{10,11... | collective-permute-start | bytes 786440 | tf_op jit(solution)/shard_map/ppermute | solution.py:82
  50.4 6.5 %collective-permute-start.16 = (bf16[4,256,128]{2,1,0:T(8,128)(2,1)S(1)}, bf16[4,256,128]{2,1,0:T(8,128)(2,1)S(1)}, u32[]{:S(2)}, u32[]{:S(2)}) collective-permute-start(bf16[4,256,128]{2,1,0:T(8,128)(2,1)S(1)} %add_convert_fusion.1), channel_id=1, source_target_pairs={{0,16},{1,17},{2,18},{3,19},{4,20},{5,21},{6,22},{7,23},{8,56},{9,... | collective-permute-start | bytes 786440 | tf_op jit(solution)/shard_map/ppermute | solution.py:82
  57.0 11.6 %collective-permute-start.21 = (bf16[2,128,256]{2,1,0:T(8,128)(2,1)S(1)}, bf16[2,128,256]{2,1,0:T(8,128)(2,1)S(1)}, u32[]{:S(2)}, u32[]{:S(2)}) collective-permute-start(bf16[2,128,256]{2,1,0:T(8,128)(2,1)S(1)} %slice.58), channel_id=1, source_target_pairs={{0,1},{1,0},{2,3},{3,2},{4,5},{5,4},{6,7},{7,6},{8,11},{9,10},{10,... | collective-permute-start | bytes 393224 | tf_op jit(solution)/shard_map/ppermute | solution.py:82
  60.9 7.9 %collective-permute-start.18 = (bf16[1,256,128]{2,1,0:T(8,128)(2,1)S(1)}, bf16[1,256,128]{2,1,0:T(8,128)(2,1)S(1)}, u32[]{:S(2)}, u32[]{:S(2)}) collective-permute-start(bf16[1,256,128]{2,1,0:T(8,128)(2,1)S(1)} %get-tuple-element.93), channel_id=1, source_target_pairs={{0,192},{1,193},{2,194},{3,195},{4,196},{5,197},{6,198},{7,199},{8... | collective-permute-start | bytes 196616 | tf_op jit(solution)/shard_map/ppermute | solution.py:82
  66.2 5.4 %collective-permute-start.19 = (bf16[1,256,128]{2,1,0:T(8,128)(2,1)S(1)}, bf16[1,256,128]{2,1,0:T(8,128)(2,1)S(1)}, u32[]{:S(2)}, u32[]{:S(2)}) collective-permute-start(bf16[1,256,128]{2,1,0:T(8,128)(2,1)S(1)} %get-tuple-element.92), channel_id=1, source_target_pairs={{0,4},{1,5},{2,6},{3,7},{4,0},{5,1},{6,2},{7,3},{8,12},{9,13},{10,... | collective-permute-start | bytes 196616 | tf_op jit(solution)/shard_map/ppermute | solution.py:82
  68.6 6.2 %collective-permute-start.20 = (bf16[1,256,128]{2,1,0:T(8,128)(2,1)S(1)}, bf16[1,256,128]{2,1,0:T(8,128)(2,1)S(1)}, u32[]{:S(2)}, u32[]{:S(2)}) collective-permute-start(bf16[1,256,128]{2,1,0:T(8,128)(2,1)S(1)} %get-tuple-element.91), channel_id=1, source_target_pairs={{0,196},{1,197},{2,198},{3,199},{4,192},{5,193},{6,194},{7,195},{8... | collective-permute-start | bytes 196616 | tf_op jit(solution)/shard_map/ppermute | solution.py:82
  68.7 6.1 %collective-permute-start.22 = (bf16[1,128,256]{2,1,0:T(8,128)(2,1)S(1)}, bf16[1,128,256]{2,1,0:T(8,128)(2,1)S(1)}, u32[]{:S(2)}, u32[]{:S(2)}) collective-permute-start(bf16[1,128,256]{2,1,0:T(8,128)(2,1)S(1)} %slice.59), channel_id=1, source_target_pairs={{0,64},{1,65},{2,66},{3,67},{4,68},{5,69},{6,70},{7,71},{8,72},{9,... | collective-permute-start | bytes 196616 | tf_op jit(solution)/shard_map/ppermute | solution.py:82
